TPU v7x, 512 devices: a whole 4x4x16 slice. The times are simulated.
512 devices in a mesh: dp: 64 (over z_lo, x, y), tensor: 8 (over z_hi, core).
Axes of the slice: x: 4, y: 4, z: 16 (z_hi: 4, z_lo: 4; z = z_hi * 4 + z_lo), core: 2. Of those that a mesh axis runs over, the one named last changes fastest.
Arguments:
- tokens: bfloat16 [16384, 8192], P('dp', 'tensor'), may hold values from -6 to 6
- frozen: bfloat16 [1024, 8192], P('dp', 'tensor'), may hold values from -1 to 1
- down_factor: bfloat16 [32, 8192], P(None, 'tensor'), may hold values from -0.125 to 0.125
- up_factor: bfloat16 [2, 16, 512], replicated, may hold values from -0.75 to 0.75
- magnitude: float32 [1024], replicated, may hold values from 0.5 to 2
- key_value_gradient: bfloat16 [16384, 1024], P(('dp', 'tensor')), may hold values from -6 to 6
Outputs:
- projected: bfloat16 [16384, 1024], P(('dp', 'tensor'))
- token_gradient: bfloat16 [16384, 8192], P('dp', 'tensor')
- down_factor_gradient: float32 [32, 8192], P(None, 'tensor')
- up_factor_gradient: float32 [2, 16, 512], replicated
- magnitude_gradient: float32 [1024], replicated
All inputs are finite; a program needn't handle non-finite values.
Results may differ from a plain program's by a relative error of at most 0.0055.
Values may be sent and summed in bfloat16 or wider, within the bound.
A program may use at most 64 MiB of HBM per device.

v0:
```python
import math

import jax
import jax.numpy as jnp
from jax import lax
from jax.sharding import PartitionSpec as P

stability_eps = 1e-06


def upward_block(up_factor):
    reduced_rank_update = up_factor.shape[1]
    halfway_columns = up_factor.shape[2]
    zeroed_block = jnp.zeros((reduced_rank_update, halfway_columns), up_factor.dtype)
    top_half = jnp.concatenate([up_factor[0], zeroed_block], axis=1)
    bottom_half = jnp.concatenate([zeroed_block, up_factor[1]], axis=1)
    return jnp.concatenate([top_half, bottom_half], axis=0)


def squared_rows(weight_row_slice, down_factor, up_factor_cols):
    count = weight_row_slice.shape[0]
    step = min(256, count)
    down_wide = down_factor.astype(jnp.float32)
    rows3 = weight_row_slice.reshape(count // step, step, weight_row_slice.shape[1])
    cols3 = up_factor_cols.astype(jnp.float32).reshape(count // step, step, up_factor_cols.shape[1])

    def one_block(pair):
        fixed_weight_rows, down_factor_rows = pair
        combined_weight = fixed_weight_rows.astype(jnp.float32) + jnp.dot(
            down_factor_rows, down_wide, precision=lax.Precision.HIGHEST
        )
        return jnp.sum(combined_weight * combined_weight, axis=1)

    return lax.map(one_block, (rows3, cols3)).reshape(count)


def body(tokens, frozen, down_factor, up_factor, magnitude, key_value_gradient):
    reduced_rank_update = up_factor.shape[1]
    halfway_columns = up_factor.shape[2]
    upper_factor_block = upward_block(up_factor)
    up_wide = upper_factor_block.astype(jnp.float32)
    complete_weight = lax.all_gather(frozen, "dp", axis=0, tiled=True)
    partial_squares = squared_rows(complete_weight, down_factor, upper_factor_block.T)
    norm_sq = lax.psum(partial_squares, "tensor")
    column_norm = jnp.sqrt(norm_sq + stability_eps)
    factor = magnitude / column_norm
    low_part = lax.dot_general(
        tokens, down_factor, (((1,), (1,)), ((), ())), preferred_element_type=jnp.float32
    )
    partial_out = lax.dot_general(
        tokens, complete_weight, (((1,), (1,)), ((), ())), preferred_element_type=jnp.float32
    )
    partial_out = partial_out + jnp.dot(low_part, up_wide, precision=lax.Precision.HIGHEST)
    summed = lax.psum_scatter(partial_out * factor, "tensor", scatter_dimension=0, tiled=True)
    projected = summed.astype(jnp.bfloat16)
    ratio = summed / magnitude
    scaled_mine = (key_value_gradient.astype(jnp.float32) * factor).astype(jnp.bfloat16)
    scaled_all = lax.all_gather(scaled_mine, "tensor", axis=0, tiled=True)
    reduced_gradient = lax.dot_general(
        scaled_all, upper_factor_block, (((1,), (1,)), ((), ())), preferred_element_type=jnp.float32
    ).astype(jnp.bfloat16)
    input_gradient = jnp.dot(
        scaled_all,
        lax.all_gather(frozen, "dp", axis=0, tiled=True),
        preferred_element_type=jnp.float32,
    )
    token_gradient = (
        input_gradient + jnp.dot(reduced_gradient, down_factor, preferred_element_type=jnp.float32)
    ).astype(jnp.bfloat16)
    low_full = lax.psum(low_part, "tensor")
    low_q = low_full.astype(jnp.bfloat16)
    local_a = lax.dot_general(
        reduced_gradient, tokens, (((0,), (0,)), ((), ())), preferred_element_type=jnp.float32
    )
    complete_up_factor = lax.dot_general(
        low_q, scaled_all, (((0,), (0,)), ((), ())), preferred_element_type=jnp.float32
    )
    local_b = jnp.stack(
        [
            complete_up_factor[:reduced_rank_update, :halfway_columns],
            complete_up_factor[reduced_rank_update:, halfway_columns:],
        ]
    )
    local_m = jnp.sum(key_value_gradient.astype(jnp.float32) * ratio, axis=0)
    summed_a, summed_b = lax.psum((local_a, local_b), "dp")
    summed_m = lax.psum(local_m, ("dp", "tensor"))
    reciprocal_root = 1.0 / math.sqrt(tokens.shape[0] * lax.axis_size("dp"))
    return (
        projected,
        token_gradient,
        summed_a * reciprocal_root,
        summed_b * reciprocal_root,
        summed_m * reciprocal_root,
    )


def solution(mesh):
    placed = (
        P("dp", "tensor"),
        P("dp", "tensor"),
        P(None, "tensor"),
        P(),
        P(),
        P(("dp", "tensor"), None),
    )
    return jax.shard_map(
        body,
        mesh=mesh,
        in_specs=placed,
        out_specs=(P(("dp", "tensor"), None), P("dp", "tensor"), P(None, "tensor"), P(), P()),
        check_vma=False,
    )
```

profile of v0, /device:TPU:1, one launch (start us, length us, event | category | flops | bytes accessed | tf_op | source)
XLA Modules:
  0.0 1237.6 jit_solution(7843004924566870750)
XLA Ops:
  7.2 0.0 copy-start
  7.2 0.0 all-gather.2.cloned.1.call-start
  7.2 0.7 all-gather.2.cloned.1.call-update
  7.9 0.0 reduce-scatter.2.cloned.1.call-start
  8.0 0.9 convert_element_type.34
  8.8 0.7 slice_bitcast_fusion.3
  9.6 0.2 copy.11
  9.8 0.0 copy-done
  9.8 1.1 fusion.17
  10.9 315.0 %all-gather.2.cloned.1.call-done = bf16[1024,1024]{1,0:T(8,128)(2,1)} async-done(((bf16[16,1024]{1,0:T(8,128)(2,1)}), bf16[1024,1024]{1,0:T(8,128)(2,1)}) %all-gather.2.cloned.1.call-update) | async-done | bytes 2097168 | tf_op jit(solution)/shard_map/all_gather | solution.py:42
  325.9 0.0 copy-start.4
  325.9 8.7 while.10
  325.9 2.1 fusion.41
  328.1 2.1 fusion.41
  330.2 2.1 fusion.41
  332.4 2.1 fusion.41
  334.6 79.4 %all-reduce.3 = (f32[1024]{0:T(1024)S(1)}, bf16[256,32]{0,1:T(8,128)(2,1)S(1)}) all-reduce(f32[1024]{0:T(1024)S(1)} %bitcast.49, f32[256,32]{0,1:T(8,128)S(1)} %fusion.17), channel_id=1, replica_groups=mesh['dp'=64,'tensor'=8] {'tensor'}, use_global_device_ids=true, to_apply=%region_3.4 | all-reduce | flops 9216 | bytes 57344 | tf_op jit(solution)/shard_map/psum | solution.py:44
  414.0 0.0 copy-done.4
  414.0 2.3 fusion.16
  416.3 0.0 copy-start.3
  416.3 1.7 fusion.5
  418.0 0.0 copy-start.1
  418.0 0.0 reduce-scatter.2.cloned.1.call-update
  418.0 0.0 all-reduce.6.cloned.1.call-start
  418.1 51.8 %reduce-scatter.2.cloned.1.call-done = f32[32,1024]{1,0:T(8,128)} async-done(((f32[256,1024]{1,0:T(8,128)}), f32[32,1024]{1,0:T(8,128)}) %reduce-scatter.2.cloned.1.call-update) | async-done | bytes 131088 | tf_op jit(solution)/shard_map/reduce_scatter | solution.py:54
  469.9 0.0 copy-done.3
  469.9 1.6 fusion.8
  471.5 105.9 %psum.39 = f32[1024]{0:T(1024)S(1)} all-reduce(f32[1024]{0:T(1024)S(1)} %get-tuple-element.47), channel_id=1, replica_groups=mesh['dp'=64,'tensor'=8] {'dp','tensor'}, use_global_device_ids=true, to_apply=%region_9.10 | all-reduce | flops 1024 | bytes 8192 | tf_op jit(solution)/shard_map/psum | solution.py:86
  577.5 20.7 %all_gather.8 = bf16[256,1024]{1,0:T(8,128)(2,1)S(1)} all-gather(bf16[32,1024]{1,0:T(8,128)(2,1)S(1)} %get-tuple-element.51), channel_id=1, replica_groups=mesh['dp'=64,'tensor'=8] {'tensor'}, dimensions={0}, use_global_device_ids=true | all-gather | bytes 589824 | tf_op jit(solution)/shard_map/all_gather | solution.py:58
  598.2 0.2 convolution_convert_fusion
  598.4 0.0 copy-start.2
  598.4 0.9 fusion.19
  599.3 0.0 copy-done.1
  599.3 0.7 fusion.18
  600.0 0.0 copy-done.2
  600.0 1.1 fusion.6
  601.1 0.2 fusion.20
  601.3 0.6 pad_maximum_fusion
  602.0 0.0 all-reduce.6.cloned.1.call-update
  602.0 0.6 broadcast_multiply_fusion.2
  602.6 625.5 %all-reduce.6.cloned.1.call-done = (f32[32,1024]{1,0:T(8,128)}, f32[2,16,512]{2,1,0:T(8,128)}) async-done(((f32[32,1024]{1,0:T(8,128)}, f32[2,16,512]{2,1,0:T(8,128)}), (f32[32,1024]{1,0:T(8,128)}, f32[2,16,512]{2,1,0:T(8,128)})) %all-reduce.6.cloned.1.call-update) | async-done | bytes 196624 | tf_op jit(solution)/shard_map/psum | solution.py:85
  1228.1 1.6 broadcast_multiply_fusion
  1229.6 1.5 broadcast_multiply_fusion.1
  (9 shorter events, 0.2 us)
Async XLA Ops:
  7.2 2.6 copy-start
  7.2 318.7 %all-gather.2.cloned.1.call-start = ((), (), s32[]{:S(2)}) async-start(), calls=%async_computation.1 | async-start | bytes 2129920 | tf_op jit(solution)/shard_map/all_gather | solution.py:42
  7.9 462.0 %reduce-scatter.2.cloned.1.call-start = ((), (), s32[]{:S(2)}) async-start(), calls=%async_computation.2 | async-start | bytes 1179648 | tf_op jit(solution)/shard_map/reduce_scatter | solution.py:54
  325.9 88.1 %copy-start.4 = (f32[1024]{0:T(1024)S(1)}, f32[1024]{0:T(1024)}, u32[]{:S(2)}) copy-start(f32[1024]{0:T(1024)} %param.12) | copy-start | bytes 12292
  416.3 53.6 %copy-start.3 = (bf16[32,1024]{1,0:T(8,128)(2,1)S(1)}, bf16[32,1024]{1,0:T(8,128)(2,1)}, u32[]{:S(2)}) copy-start(bf16[32,1024]{1,0:T(8,128)(2,1)} %param.13) | copy-start | bytes 196612
  418.0 181.3 %copy-start.1 = (bf16[4,256,1024]{2,1,0:T(8,128)(2,1)S(1)}, bf16[4,256,1024]{2,1,0:T(8,128)(2,1)}, u32[]{:S(2)}) copy-start(bf16[4,256,1024]{2,1,0:T(8,128)(2,1)} %get-tuple-element.113) | copy-start | bytes 6291460
  418.0 810.0 %all-reduce.6.cloned.1.call-start = ((), (), s32[]{:S(2)}) async-start(), calls=%async_computation.3 | async-start | bytes 393216 | tf_op jit(solution)/shard_map/psum | solution.py:85
  598.4 1.6 copy-start.2
Sparse Core Ops, SparseCore 0:
  10.1 315.7 all-gather.1
  418.2 51.7 reduce-scatter.1
  602.1 625.8 all-reduce.5
where the time goes:
time: 1260 us; the launch traced here: 1240 us
  waiting for transfers between devices  993 us (79%)
  blocking collectives  206 us (16%)
  matrix products  16.7 us (1%)
  between operations  13.9 us (1%)
    psum x1, waiting for transfers between devices, body(): summed_a, summed_b = lax.psum((local_a, local_b), 'dp')  625 us
    all_gather x1, waiting for transfers between devices, body(): complete_weight = lax.all_gather(frozen, 'dp', axis=0, tiled=True)  315 us
    psum x1, blocking collectives, body(): summed_m = lax.psum(local_m, ('dp', 'tensor'))  106 us
    psum x1, blocking collectives, body(): norm_sq = lax.psum(partial_squares, 'tensor')  79.4 us
    reduce_scatter x1, waiting for transfers between devices, body(): lax.psum_scatter(partial_out * factor, 'tensor', scatter_dimension=0, til...  51.8 us
  transfers between devices with their start and end apart: 3, of which 3 were waited for; matrix products, arithmetic and copies ran while one was open for 0% of the time, Pallas kernels for 0%

commit v1 on v0

v1 whole, which is shorter than its diff:
```python
import functools
import math

import jax
import jax.numpy as jnp
from jax import lax
from jax.experimental import pallas as pl
from jax.experimental.pallas import tpu as pltpu
from jax.sharding import PartitionSpec as P

stability_eps = 1e-06
MESH = pl.DeviceIdType.MESH
F32 = jnp.float32
BF16 = jnp.bfloat16
OFFSETS = (0, 3, 1, 2)


def nt(a, b):
    return lax.dot_general(a, b, (((1,), (1,)), ((), ())), preferred_element_type=F32)


def nn(a, b):
    return jnp.dot(a, b, preferred_element_type=F32)


def kernel(
    scale,
    tok,
    fro,
    dwn,
    upf,
    mag,
    kvg,
    proj,
    tg,
    da,
    db,
    mgo,
    weight,
    cot,
    up,
    part,
    grad,
    swap_out,
    swap_in,
    hop_out,
    hop_in,
    norm_t,
    norm_z,
    norm_x,
    norm_y,
    mgrad,
    fac,
    inv,
    gpart,
    gplane,
    gdepth,
    gtens,
    gfull,
    f_send,
    f_recv,
    k_send,
    k_recv,
    n_send,
    nt_recv,
    nz_recv,
    nx_recv,
    ny_recv,
    c_send,
    c_recv,
    g1_send,
    g2_send,
    g3_send,
    g4_send,
    g1_recv,
    g2_recv,
    g3_recv,
    g4_recv,
):
    dp = lax.axis_index("dp")
    t = lax.axis_index("tensor")
    rem = lax.rem
    z, p = lax.div(dp, 16), rem(dp, 16)
    x, y = lax.div(p, 4), rem(p, 4)
    h, c = lax.div(t, 2), rem(t, 2)
    sib = (dp, h * 2 + 1 - c)
    sends = []

    def at(zz, xx, yy):
        return ((zz * 4 + xx) * 4 + yy, t)

    def plane(q):
        return (z * 16 + q, t)

    def tens(hh, cc):
        return (dp, hh * 2 + cc)

    def send(src, dst, ssem, rsem, dev):
        d = pltpu.make_async_remote_copy(
            src_ref=src,
            dst_ref=dst,
            send_sem=ssem,
            recv_sem=rsem,
            device_id=dev,
            device_id_type=MESH,
        )
        d.start()
        sends.append(d)

    def arrived(dst, rsem):
        pltpu.make_async_remote_copy(
            src_ref=dst,
            dst_ref=dst,
            send_sem=f_send.at[0],
            recv_sem=rsem,
            device_id=sib,
            device_id_type=MESH,
        ).wait_recv()

    def spread(buf, own, n, peer, ssem, base, rsem):
        for k in range(1, n):
            send(
                buf.at[own], buf.at[own], ssem.at[base + k - 1], rsem.at[own],
                peer(rem(own + k, n)),
            )

    def collect(buf, own, n, rsem):
        for k in range(1, n):
            q = rem(own + k, n)
            arrived(buf.at[q], rsem.at[q])

    def total(buf, n):
        acc = buf[0].astype(F32)
        for i in range(1, n):
            acc = acc + buf[i].astype(F32)
        return acc

    barrier = pltpu.get_barrier_semaphore()

    def greet(dev):
        pl.semaphore_signal(barrier, inc=1, device_id=dev, device_id_type=MESH)

    for k in range(1, 16):
        greet(plane(rem(p + k, 16)))
    for k in range(1, 4):
        greet(at(rem(z + k, 4), x, y))
    for k in range(1, 8):
        greet((dp, rem(t + k, 8)))
    pl.semaphore_wait(barrier, 25)

    for k in range(1, 4):
        send(fro, weight.at[z, x, y], f_send.at[k - 1], f_recv.at[z], at(rem(z + k, 4), x, y))
    up_h, down_h = rem(h + 1, 4), rem(h + 3, 4)
    fwd = rem(h + 1 + 2 * c, 4)
    bwd = rem(h + 3 + 2 * c, 4)
    far = rem(h + 2, 4)
    send(kvg, cot.at[t], k_send.at[0], k_recv.at[0], tens(up_h, c))
    send(kvg, cot.at[t], k_send.at[1], k_recv.at[1], tens(down_h, c))
    send(kvg, cot.at[t], k_send.at[2], k_recv.at[3], sib)
    weight[z, x, y] = fro[...]
    cot[t] = kvg[...]

    up[...] = jnp.zeros_like(up)
    up[0:16, 0:512] = upf[0]
    up[16:32, 512:1024] = upf[1]
    row = lax.broadcasted_iota(jnp.int32, (16, 1024), 0)
    col = lax.broadcasted_iota(jnp.int32, (16, 1024), 1)
    pick = jnp.where(col == row + dp * 16, 1.0, 0.0).astype(BF16)
    mine = nt(pick, up[...]).astype(BF16)
    merged = fro[...].astype(F32) + nn(mine, dwn[...])
    squares = jnp.sum(merged * merged, axis=1, keepdims=True)
    row = lax.broadcasted_iota(jnp.int32, (16, 128), 0)
    col = lax.broadcasted_iota(jnp.int32, (16, 128), 1)
    line = jnp.sum(
        jnp.where(col == row + rem(dp, 8) * 16, squares, 0.0), axis=0, keepdims=True
    )
    row = lax.broadcasted_iota(jnp.int32, (8, 128), 0)
    norm_t[t] = jnp.where(row == lax.div(dp, 8), line, 0.0)
    spread(norm_t, t, 8, lambda q: (dp, q), n_send, 0, nt_recv)

    def unit(half, i, j):
        return weight.at[pl.ds(0, 2), i, j] if half == 0 else weight.at[pl.ds(2, 2), j, i]

    def piece(half, which, i, j):
        return weight.at[which, i, j] if half == 0 else weight.at[2 + which, j, i]

    def dev(half, i, j):
        return at(z, i, j) if half == 0 else at(z, j, i)

    pos = ((x, y), (y, x))

    def sem(half, group, kind):
        return 4 + half * 20 + group * 4 + kind

    def first(half):
        i, j = pos[half]
        for kind, step in ((0, 1), (1, 3)):
            s = sem(half, 0, kind)
            send(unit(half, i, j), unit(half, i, j), f_send.at[s], f_recv.at[s],
                 dev(half, rem(i + step, 4), j))

    def first_relay(half):
        i, j = pos[half]
        for kind, step in ((0, 1), (1, 3)):
            src = rem(i + 4 - step, 4)
            arrived(unit(half, src, j), f_recv.at[sem(half, 0, kind)])
            s = sem(half, 0, 2 + kind)
            send(piece(half, kind, src, j), piece(half, kind, src, j), f_send.at[s],
                 f_recv.at[s], dev(half, rem(i + step, 4), j))

    def first_done(half):
        i, j = pos[half]
        for kind in range(2):
            arrived(piece(half, kind, rem(i + 2, 4), j), f_recv.at[sem(half, 0, 2 + kind)])

    def second(half, g):
        i, j = pos[half]
        u = rem(i + OFFSETS[g], 4)
        for kind, step in ((0, 1), (1, 3)):
            s = sem(half, 1 + g, kind)
            send(unit(half, u, j), unit(half, u, j), f_send.at[s], f_recv.at[s],
                 dev(half, i, rem(j + step, 4)))

    def second_relay(half, g):
        i, j = pos[half]
        u = rem(i + OFFSETS[g], 4)
        for kind, step in ((0, 1), (1, 3)):
            src = rem(j + 4 - step, 4)
            arrived(unit(half, u, src), f_recv.at[sem(half, 1 + g, kind)])
            s = sem(half, 1 + g, 2 + kind)
            send(piece(half, kind, u, src), piece(half, kind, u, src), f_send.at[s],
                 f_recv.at[s], dev(half, i, rem(j + step, 4)))

    def second_done(half, g):
        i, j = pos[half]
        u = rem(i + OFFSETS[g], 4)
        for kind in range(2):
            arrived(piece(half, kind, u, rem(j + 2, 4)),
                    f_recv.at[sem(half, 1 + g, 2 + kind)])

    for k in range(1, 4):
        q = rem(z + k, 4)
        arrived(weight.at[q, x, y], f_recv.at[q])
    for half in range(2):
        first(half)
    for half in range(2):
        second(half, 0)

    collect(norm_t, t, 8, nt_recv)
    norm_z[z] = total(norm_t, 8)
    spread(norm_z, z, 4, lambda q: at(q, x, y), n_send, 7, nz_recv)

    for half in range(2):
        first_relay(half)
    for half in range(2):
        second(half, 1)
        second(half, 2)

    collect(norm_z, z, 4, nz_recv)
    norm_x[x] = total(norm_z, 4)
    spread(norm_x, x, 4, lambda q: at(z, q, y), n_send, 10, nx_recv)

    for half in range(2):
        second_relay(half, 0)
    for half in range(2):
        first_done(half)
        second(half, 3)

    low = nt(tok[...], dwn[...])
    low_hi = low.astype(BF16)
    low_lo = (low - low_hi.astype(F32)).astype(BF16)
    low_t = nt(dwn[...], tok[...])
    low_t_hi = low_t.astype(BF16)
    low_t_lo = (low_t - low_t_hi.astype(F32)).astype(BF16)

    arrived(cot.at[bwd * 2 + c], k_recv.at[c])
    send(cot.at[bwd * 2 + c], cot.at[bwd * 2 + c], k_send.at[3], k_recv.at[2], tens(fwd, c))
    send(cot.at[bwd * 2 + c], cot.at[bwd * 2 + c], k_send.at[4], k_recv.at[4], sib)

    collect(norm_x, x, 4, nx_recv)
    norm_y[y] = total(norm_x, 4)
    spread(norm_y, y, 4, lambda q: at(z, x, q), n_send, 13, ny_recv)

    arrived(cot.at[fwd * 2 + c], k_recv.at[1 - c])
    send(cot.at[fwd * 2 + c], cot.at[fwd * 2 + c], k_send.at[5], k_recv.at[5], sib)

    for half in range(2):
        second_relay(half, 1)
    for half in range(2):
        second_relay(half, 2)

    collect(norm_y, y, 4, ny_recv)
    norm = jnp.sqrt(total(norm_y, 4) + stability_eps)
    fac[...] = mag[...] / norm
    inv[...] = 1.0 / norm

    for half in range(2):
        second_relay(half, 3)

    arrived(cot.at[far * 2 + c], k_recv.at[2])
    send(cot.at[far * 2 + c], cot.at[far * 2 + c], k_send.at[6], k_recv.at[6], sib)
    arrived(cot.at[h * 2 + 1 - c], k_recv.at[3])
    arrived(cot.at[fwd * 2 + 1 - c], k_recv.at[4])
    arrived(cot.at[bwd * 2 + 1 - c], k_recv.at[5])
    arrived(cot.at[far * 2 + 1 - c], k_recv.at[6])

    for i in range(8):
        cols = pl.ds(i * 128, 128)
        grad[:, cols] = (
            cot[:, :, cols].reshape(256, 128).astype(F32) * fac[i : i + 1, :]
        ).astype(BF16)
    low_grad = nt(grad[...], up[...]).astype(BF16)
    low_grad_t = nt(up[...], grad[...]).astype(BF16)
    grad_a = nn(low_grad_t, tok[...])
    grad_b = nn(low_t_hi, grad[...]) + nn(low_t_lo, grad[...])

    for half in range(2):
        for g in range(4):
            second_done(half, g)

    for j in range(4):
        cols = pl.ds(j * 256, 256)
        rows = weight[j].reshape(256, 1024)
        out = nt(tok[...], rows) + nn(low_hi, up[:, cols]) + nn(low_lo, up[:, cols])
        part[:, :, :, cols] = out.reshape(4, 2, 32, 256)
        swap_out[j] = part[:, 1 - c, :, cols].astype(BF16)
        send(swap_out.at[j], swap_in.at[j], c_send.at[j], c_recv.at[j], sib)
        m = jnp.sum(
            cot[:, :, cols].reshape(256, 256).astype(F32) * out, axis=0, keepdims=True
        )
        mgrad[2 * j : 2 * j + 1, :] = m[:, 0:128]
        mgrad[2 * j + 1 : 2 * j + 2, :] = m[:, 128:256]

    mg = mgrad[...] * inv[...]
    for q in range(16):
        r, b = q // 8, q % 8
        gb = grad_b[8 * r : 8 * r + 8] if b < 4 else grad_b[16 + 8 * r : 24 + 8 * r]
        gpart[q] = jnp.concatenate(
            [
                grad_a[16 * r : 16 * r + 16, 128 * b : 128 * b + 128],
                gb[:, 128 * b : 128 * b + 128],
                jnp.broadcast_to(mg[b : b + 1, :], (8, 128)),
            ],
            axis=0,
        ).astype(BF16)
    for k in range(1, 16):
        q = rem(p + k, 16)
        send(gpart.at[q], gplane.at[p], g1_send.at[k - 1], g1_recv.at[p], plane(q))
    gplane[p] = gpart[p]

    for j in range(4):
        cols = pl.ds(j * 256, 256)
        arrived(swap_in.at[j], c_recv.at[j])
        both = part[:, c, :, cols] + swap_in[j].astype(F32)
        part[:, c, :, cols] = both
        hop_out[j, 0] = part[far, c, :, cols].astype(BF16)
        send(hop_out.at[j, 0], hop_in.at[j, 0], c_send.at[4 + j], c_recv.at[4 + j],
             tens(fwd, c))
        hop_out[j, 1] = part[bwd, c, :, cols].astype(BF16)
        send(hop_out.at[j, 1], hop_in.at[j, 1], c_send.at[8 + j], c_recv.at[8 + j],
             tens(bwd, c))

    for j in range(4):
        cols = pl.ds(j * 256, 256)
        rows = weight[:, :, :, :, cols].reshape(1024, 256)
        tg[:, cols] = (nn(grad[...], rows) + nn(low_grad, dwn[:, cols])).astype(BF16)

    collect(gplane, p, 16, g1_recv)
    gdepth[z] = total(gplane, 16)
    spread(gdepth, z, 4, lambda q: at(q, x, y), g2_send, 0, g2_recv)

    for j in range(4):
        cols = pl.ds(j * 256, 256)
        arrived(hop_in.at[j, 0], c_recv.at[4 + j])
        hop_out[j, 2] = (part[fwd, c, :, cols] + hop_in[j, 0].astype(F32)).astype(BF16)
        send(hop_out.at[j, 2], hop_in.at[j, 2], c_send.at[12 + j], c_recv.at[12 + j],
             tens(fwd, c))

    collect(gdepth, z, 4, g2_recv)
    deep = total(gdepth, 4)
    gtens[t] = deep[16:32]
    spread(gtens, t, 8, lambda q: (dp, q), g3_send, 0, g3_recv)
    collect(gtens, t, 8, g3_recv)
    gfull[p] = jnp.concatenate([deep[0:16], total(gtens, 8)], axis=0).astype(BF16)
    spread(gfull, p, 16, plane, g4_send, 0, g4_recv)

    for j in range(4):
        cols = pl.ds(j * 256, 256)
        arrived(hop_in.at[j, 1], c_recv.at[8 + j])
        arrived(hop_in.at[j, 2], c_recv.at[12 + j])
        summed = (
            part[h, c, :, cols] + hop_in[j, 1].astype(F32) + hop_in[j, 2].astype(F32)
        )
        f = jnp.concatenate([fac[2 * j : 2 * j + 1, :], fac[2 * j + 1 : 2 * j + 2, :]], axis=1)
        proj[:, cols] = (summed * f).astype(BF16)

    collect(gfull, p, 16, g4_recv)
    for q in range(16):
        r, b = q // 8, q % 8
        got = gfull[q].astype(F32) * scale
        da[16 * r : 16 * r + 16, 128 * b : 128 * b + 128] = got[0:16]
        lo = 128 * (b % 4)
        db[b // 4, 8 * r : 8 * r + 8, lo : lo + 128] = got[16:24]
        if r == 0:
            mgo[b : b + 1, :] = got[24:25]

    for d in sends:
        d.wait_send()


def body(tokens, frozen, down_factor, up_factor, magnitude, key_value_gradient):
    scale = 1.0 / math.sqrt(tokens.shape[0] * lax.axis_size("dp"))
    dma = pltpu.SemaphoreType.DMA
    vmem = pl.BlockSpec(memory_space=pltpu.VMEM)
    projected, token_gradient, grad_a, grad_b, grad_m = pl.pallas_call(
        functools.partial(kernel, scale),
        out_shape=(
            jax.ShapeDtypeStruct((32, 1024), BF16),
            jax.ShapeDtypeStruct((256, 1024), BF16),
            jax.ShapeDtypeStruct((32, 1024), F32),
            jax.ShapeDtypeStruct((2, 16, 512), F32),
            jax.ShapeDtypeStruct((8, 128), F32),
        ),
        in_specs=[vmem] * 6,
        out_specs=(vmem,) * 5,
        scratch_shapes=[
            pltpu.VMEM((4, 4, 4, 16, 1024), BF16),
            pltpu.VMEM((8, 32, 1024), BF16),
            pltpu.VMEM((32, 1024), BF16),
            pltpu.VMEM((4, 2, 32, 1024), F32),
            pltpu.VMEM((256, 1024), BF16),
            pltpu.VMEM((4, 4, 32, 256), BF16),
            pltpu.VMEM((4, 4, 32, 256), BF16),
            pltpu.VMEM((4, 3, 32, 256), BF16),
            pltpu.VMEM((4, 3, 32, 256), BF16),
            pltpu.VMEM((8, 8, 128), F32),
            pltpu.VMEM((4, 8, 128), F32),
            pltpu.VMEM((4, 8, 128), F32),
            pltpu.VMEM((4, 8, 128), F32),
            pltpu.VMEM((8, 128), F32),
            pltpu.VMEM((8, 128), F32),
            pltpu.VMEM((8, 128), F32),
            pltpu.VMEM((16, 32, 128), BF16),
            pltpu.VMEM((16, 32, 128), BF16),
            pltpu.VMEM((4, 32, 128), F32),
            pltpu.VMEM((8, 16, 128), F32),
            pltpu.VMEM((16, 32, 128), BF16),
            dma((44,)),
            dma((44,)),
            dma((7,)),
            dma((7,)),
            dma((16,)),
            dma((8,)),
            dma((4,)),
            dma((4,)),
            dma((4,)),
            dma((16,)),
            dma((16,)),
            dma((15,)),
            dma((3,)),
            dma((7,)),
            dma((15,)),
            dma((16,)),
            dma((4,)),
            dma((8,)),
            dma((16,)),
        ],
        compiler_params=pltpu.CompilerParams(
            collective_id=0, has_side_effects=True, vmem_limit_bytes=32 * 1024 * 1024
        ),
        cost_estimate=pl.CostEstimate(
            flops=1200000000, bytes_accessed=2000000, transcendentals=0
        ),
    )(
        tokens,
        frozen,
        down_factor,
        up_factor,
        magnitude.reshape(8, 128),
        key_value_gradient,
    )
    return projected, token_gradient, grad_a, grad_b, grad_m.reshape(1024)


def solution(mesh):
    placed = (
        P("dp", "tensor"),
        P("dp", "tensor"),
        P(None, "tensor"),
        P(),
        P(),
        P(("dp", "tensor"), None),
    )
    return jax.shard_map(
        body,
        mesh=mesh,
        in_specs=placed,
        out_specs=(P(("dp", "tensor"), None), P("dp", "tensor"), P(None, "tensor"), P(), P()),
        check_vma=False,
    )
```

time: 1260 us -> 83.3 us (0.07); the launches traced: 1240 us -> 82.9 us
  waiting for transfers between devices: 993 us -> 0 us
  blocking collectives: 206 us -> 0 us
  Pallas kernels: 0 us -> 74 us
  matrix products: 16.7 us -> 0 us
  between operations: 13.9 us -> 0.66 us
    psum x1 -> x0, waiting for transfers between devices: 625 us -> none  [body(): summed_a, summed_b = lax.psum((local_a, local_b), 'dp')]
    all_gather x1 -> x0, waiting for transfers between devices: 315 us -> none  [body(): complete_weight = lax.all_gather(frozen, 'dp', axis=0, tiled=True)]
    psum x2 -> x0, blocking collectives: 185 us -> none  [the longest x1 106 us: body(): summed_m = lax.psum(local_m, ('dp', 'tensor'))]
    pallas_call x0 -> x1, Pallas kernels: none -> 74 us  [body(): pl.pallas_call(functools.partial(kernel, scale), out_shape=(jax.ShapeDtyp...]
    reduce_scatter x1 -> x0, waiting for transfers between devices: 51.8 us -> none  [body(): lax.psum_scatter(partial_out * factor, 'tensor', scatter_dimension=0, til...]
    all_gather x1 -> x0, blocking collectives: 20.7 us -> none  [body(): scaled_all = lax.all_gather(scaled_mine, 'tensor', axis=0, tiled=True)]
    dot_general x12 -> x0, matrix products: 16.7 us -> none  [the longest x4 8.48 us: one_block(): jnp.dot(down_factor_rows, down_wide, precision=lax.Precision.HIGHEST)]
  transfers between devices with their start and end apart: 3 -> 0, of which waited for: 3 -> 0; matrix products, arithmetic and copies ran while one was open for 0% -> 0% of each run, Pallas kernels for 0% -> 0%
where the time goes in v1:
time: 83.3 us; the launch traced here: 82.9 us
  Pallas kernels  74 us (89%)
  local copies, waits for them, and re-layouts  8.22 us (10%)
    pallas_call x1, Pallas kernels, body(): pl.pallas_call(functools.partial(kernel, scale), out_shape=(jax.ShapeDtyp...  74 us
    unnamed x17, local copies, waits for them, and re-layouts  8.22 us

profile of v1, /device:TPU:1, one launch (start us, length us, event | category | flops | bytes accessed | tf_op | source)
XLA Modules:
  0.0 82.9 jit_solution(4834853012989532770)
XLA Ops:
  0.6 0.0 copy-start
  0.6 1.0 %copy-done = bf16[256,1024]{1,0:T(8,128)(2,1)S(1)} copy-done((bf16[256,1024]{1,0:T(8,128)(2,1)S(1)}, bf16[256,1024]{1,0:T(8,128)(2,1)}, u32[]{:S(2)}) %copy-start) | copy-done | bytes 524312
  1.7 0.0 copy-start.1
  1.7 0.8 %copy-done.1 = bf16[32,1024]{1,0:T(8,128)(2,1)S(1)} copy-done((bf16[32,1024]{1,0:T(8,128)(2,1)S(1)}, bf16[32,1024]{1,0:T(8,128)(2,1)}, u32[]{:S(2)}) %copy-start.1) | copy-done | bytes 65560
  2.5 0.0 copy-start.2
  2.5 0.8 %copy-done.2 = bf16[32,1024]{1,0:T(8,128)(2,1)S(1)} copy-done((bf16[32,1024]{1,0:T(8,128)(2,1)S(1)}, bf16[32,1024]{1,0:T(8,128)(2,1)}, u32[]{:S(2)}) %copy-start.2) | copy-done | bytes 65560
  3.4 0.0 copy-start.3
  3.4 0.8 copy-done.3
  4.1 0.0 copy-start.4
  4.1 0.8 copy-done.4
  4.9 0.0 copy-start.5
  4.9 0.7 copy-done.5
  5.6 74.0 %shard_map.101 = (bf16[32,1024]{1,0:T(8,128)(2,1)S(1)}, bf16[256,1024]{1,0:T(8,128)(2,1)S(1)}, f32[32,1024]{1,0:T(8,128)S(1)}, f32[2,16,512]{2,1,0:T(8,128)S(1)}, f32[8,128]{1,0:T(8,128)S(1)}) custom-call(bf16[256,1024]{1,0:T(8,128)(2,1)S(1)} %copy-done, bf16[16,1024]{1,0:T(8,128)(2,1)S(1)} %copy-done.3, bf16[32,1024]{1,0:T(8,128)(2,1)S(1)} %copy-done.1, ...), custom_call_target="tpu_custom_call" | custom-call | flops 1200000000 | bytes 2000000 | tf_op jit(solution)/shard_map/pallas_call | solution.py:415
  79.6 0.6 copy.16
  80.2 0.8 copy.17
  81.0 0.7 copy.18
  81.7 0.6 copy.19
  82.3 0.6 copy.20
Async XLA Ops:
  0.6 1.0 %copy-start = (bf16[256,1024]{1,0:T(8,128)(2,1)S(1)}, bf16[256,1024]{1,0:T(8,128)(2,1)}, u32[]{:S(2)}) copy-start(bf16[256,1024]{1,0:T(8,128)(2,1)} %tok.1) | copy-start | bytes 1572868
  1.7 0.8 %copy-start.1 = (bf16[32,1024]{1,0:T(8,128)(2,1)S(1)}, bf16[32,1024]{1,0:T(8,128)(2,1)}, u32[]{:S(2)}) copy-start(bf16[32,1024]{1,0:T(8,128)(2,1)} %dwn.1) | copy-start | bytes 196612
  2.5 0.8 %copy-start.2 = (bf16[32,1024]{1,0:T(8,128)(2,1)S(1)}, bf16[32,1024]{1,0:T(8,128)(2,1)}, u32[]{:S(2)}) copy-start(bf16[32,1024]{1,0:T(8,128)(2,1)} %kvg.1) | copy-start | bytes 196612
  3.4 0.8 copy-start.3
  4.1 0.8 copy-start.4
  4.9 0.7 copy-start.5

commit v2 on v1

v2 whole, which is shorter than its diff:
```python
import functools
import math

import jax
import jax.numpy as jnp
from jax import lax
from jax.experimental import pallas as pl
from jax.experimental.pallas import tpu as pltpu
from jax.sharding import PartitionSpec as P

stability_eps = 1e-06
MESH = pl.DeviceIdType.MESH
F32 = jnp.float32
BF16 = jnp.bfloat16
OFFSETS = (0, 3, 1, 2)


def nt(a, b):
    return lax.dot_general(a, b, (((1,), (1,)), ((), ())), preferred_element_type=F32)


def nn(a, b):
    return jnp.dot(a, b, preferred_element_type=F32)


def kernel(
    scale,
    tok_in,
    fro,
    dwn_in,
    upf,
    mag_in,
    kvg,
    proj_out,
    tg_out,
    da_out,
    db_out,
    mg_out,
    proj,
    tg,
    da,
    db,
    mgo,
    tok,
    dwn,
    mag,
    weight,
    cot,
    up,
    part,
    pair,
    grad,
    swap_out,
    swap_in,
    hop_out,
    hop_in,
    norms,
    mags,
    facrow,
    low_swap,
    lows,
    gpart,
    gplane,
    gdepth,
    gfull,
    in_sem,
    out_sem,
    f_send,
    f_recv,
    k_send,
    k_recv,
    n_send,
    n_recv,
    m_send,
    m_recv,
    l_send,
    l_recv,
    c_send,
    c_recv,
    g1_send,
    g2_send,
    g4_send,
    g1_recv,
    g2_recv,
    g4_recv,
):
    dp = lax.axis_index("dp")
    t = lax.axis_index("tensor")
    rem = lax.rem
    z, p = lax.div(dp, 16), rem(dp, 16)
    x, y = lax.div(p, 4), rem(p, 4)
    h, c = lax.div(t, 2), rem(t, 2)
    sib = (dp, h * 2 + 1 - c)
    fwd = rem(h + 1 + 2 * c, 4)
    bwd = rem(h + 3 + 2 * c, 4)
    far = rem(h + 2, 4)
    sends = []
    writes = []

    def at(zz, xx, yy):
        return ((zz * 4 + xx) * 4 + yy, t)

    def plane(q):
        return (z * 16 + q, t)

    def depth(q):
        return at(q, x, y)

    def tens(hh):
        return (dp, hh * 2 + c)

    def send(src, dst, ssem, rsem, dev):
        d = pltpu.make_async_remote_copy(
            src_ref=src,
            dst_ref=dst,
            send_sem=ssem,
            recv_sem=rsem,
            device_id=dev,
            device_id_type=MESH,
        )
        d.start()
        sends.append(d)

    def arrived(dst, rsem):
        pltpu.make_async_remote_copy(
            src_ref=dst,
            dst_ref=dst,
            send_sem=f_send.at[0],
            recv_sem=rsem,
            device_id=sib,
            device_id_type=MESH,
        ).wait_recv()

    def spread(buf, own, n, peer, ssem, rsem, base=0, sbase=0):
        for k in range(1, n):
            send(
                buf.at[base + own], buf.at[base + own], ssem.at[sbase + k - 1],
                rsem.at[base + own], peer(rem(own + k, n)),
            )

    def collect(buf, own, n, rsem, base=0):
        for k in range(1, n):
            q = base + rem(own + k, n)
            arrived(buf.at[q], rsem.at[q])

    def total(buf, n, base=0):
        acc = buf[base].astype(F32)
        for i in range(1, n):
            acc = acc + buf[base + i].astype(F32)
        return acc

    def write(src, dst, i):
        w = pltpu.make_async_copy(src, dst, out_sem.at[i])
        w.start()
        writes.append(w)

    loads = [
        pltpu.make_async_copy(src, dst, in_sem.at[i])
        for i, (src, dst) in enumerate(
            (
                (fro, weight.at[0, x, y]),
                (dwn_in, dwn),
                (upf.at[0], up.at[pl.ds(0, 16), pl.ds(0, 512)]),
                (upf.at[1], up.at[pl.ds(16, 16), pl.ds(512, 512)]),
                (kvg, cot.at[t]),
                (tok_in, tok),
                (mag_in, mag),
            )
        )
    ]
    for load in loads:
        load.start()

    barrier = pltpu.get_barrier_semaphore()

    def greet(dev):
        pl.semaphore_signal(barrier, inc=1, device_id=dev, device_id_type=MESH)

    greet(tens(fwd))
    greet(tens(bwd))
    for k in range(1, 4):
        greet(depth(rem(z + k, 4)))
    for k in range(1, 16):
        greet(plane(rem(p + k, 16)))
    greet(sib)

    class Tile:
        def __init__(self, buf, ssem, rsem):
            self.buf, self.ssem, self.rsem = buf, ssem, rsem

        def core_send(self, value):
            self.buf[c] = value
            send(self.buf.at[c], self.buf.at[c], self.ssem.at[0], self.rsem.at[c], sib)

        def core_sum(self):
            arrived(self.buf.at[1 - c], self.rsem.at[1 - c])
            return self.buf[0] + self.buf[1]

        def ring_send(self, value):
            own = self.buf.at[2 + h]
            own[...] = value
            send(own, own, self.ssem.at[1], self.rsem.at[2 + h], tens(fwd))
            send(own, own, self.ssem.at[2], self.rsem.at[2 + h], tens(bwd))

        def ring_relay(self):
            got = self.buf.at[2 + bwd]
            arrived(got, self.rsem.at[2 + bwd])
            send(got, got, self.ssem.at[3], self.rsem.at[2 + bwd], tens(fwd))

        def ring_sum(self):
            arrived(self.buf.at[2 + fwd], self.rsem.at[2 + fwd])
            arrived(self.buf.at[2 + far], self.rsem.at[2 + far])
            return total(self.buf, 4, 2)

        def depth_send(self, value):
            self.buf[6 + z] = value
            spread(self.buf, z, 4, depth, self.ssem, self.rsem, 6, 4)

        def depth_sum(self):
            collect(self.buf, z, 4, self.rsem, 6)
            return total(self.buf, 4, 6)

        def plane_send(self, value):
            self.buf[10 + p] = value
            spread(self.buf, p, 16, plane, self.ssem, self.rsem, 10, 7)

        def plane_sum(self):
            collect(self.buf, p, 16, self.rsem, 10)
            return total(self.buf, 16, 10)

    norm_tile = Tile(norms, n_send, n_recv)
    mag_tile = Tile(mags, m_send, m_recv)

    up[0:16, 512:1024] = jnp.zeros((16, 512), BF16)
    up[16:32, 0:512] = jnp.zeros((16, 512), BF16)
    for load in loads:
        load.wait()
    row = lax.broadcasted_iota(jnp.int32, (16, 1024), 0)
    col = lax.broadcasted_iota(jnp.int32, (16, 1024), 1)
    pick = jnp.where(col == row + dp * 16, 1.0, 0.0).astype(BF16)
    mine = nt(pick, up[...]).astype(BF16)
    merged = weight[0, x, y].astype(F32) + nn(mine, dwn[...])
    squares = jnp.sum(merged * merged, axis=1, keepdims=True)
    row = lax.broadcasted_iota(jnp.int32, (16, 128), 0)
    col = lax.broadcasted_iota(jnp.int32, (16, 128), 1)
    line = jnp.sum(
        jnp.where(col == row + rem(dp, 8) * 16, squares, 0.0), axis=0, keepdims=True
    )
    row8 = lax.broadcasted_iota(jnp.int32, (8, 128), 0)
    own_squares = jnp.where(row8 == lax.div(dp, 8), line, 0.0)

    pl.semaphore_wait(barrier, 21)

    own_rows = weight.at[0, x, y]
    for k in range(1, 4):
        send(own_rows, weight.at[4 - k, x, y], f_send.at[k], f_recv.at[4 - k],
             depth(rem(z + k, 4)))
    norm_tile.core_send(own_squares)

    slots = (pl.ds(0, 1), pl.ds(1, 3))
    pos = ((x, y), (y, x))

    def block(half, grp, i, j, lo, wide):
        i, j = (i, j) if half == 0 else (j, i)
        return weight.at[slots[grp], i, j, :, pl.ds(half * 512 + lo, wide)]

    def unit(half, grp, i, j):
        return block(half, grp, i, j, 0, 512)

    def piece(half, grp, kind, i, j):
        return block(half, grp, i, j, 256 * kind, 256)

    def peer(half, i, j):
        return at(z, i, j) if half == 0 else at(z, j, i)

    def sem(half, grp, step, kind):
        return 4 + ((half * 2 + grp) * 5 + step) * 4 + kind

    def pass_on(ref, s, dev):
        send(ref, ref, f_send.at[s], f_recv.at[s], dev)

    def first(grp):
        for kind, step in ((0, 1), (1, 3)):
            for half in range(2):
                i, j = pos[half]
                pass_on(unit(half, grp, i, j), sem(half, grp, 0, kind),
                        peer(half, rem(i + step, 4), j))

    def first_relay(grp):
        for kind, step in ((0, 1), (1, 3)):
            for half in range(2):
                i, j = pos[half]
                src = rem(i + 4 - step, 4)
                arrived(unit(half, grp, src, j), f_recv.at[sem(half, grp, 0, kind)])
                pass_on(piece(half, grp, kind, src, j), sem(half, grp, 0, 2 + kind),
                        peer(half, rem(i + step, 4), j))

    def first_done(grp):
        for kind in range(2):
            for half in range(2):
                i, j = pos[half]
                arrived(piece(half, grp, kind, rem(i + 2, 4), j),
                        f_recv.at[sem(half, grp, 0, 2 + kind)])

    def second(grp, g):
        for kind, step in ((0, 1), (1, 3)):
            for half in range(2):
                i, j = pos[half]
                u = rem(i + OFFSETS[g], 4)
                pass_on(unit(half, grp, u, j), sem(half, grp, 1 + g, kind),
                        peer(half, i, rem(j + step, 4)))

    def second_relay(grp, g):
        for kind, step in ((0, 1), (1, 3)):
            for half in range(2):
                i, j = pos[half]
                u, src = rem(i + OFFSETS[g], 4), rem(j + 4 - step, 4)
                arrived(unit(half, grp, u, src), f_recv.at[sem(half, grp, 1 + g, kind)])
                pass_on(piece(half, grp, kind, u, src), sem(half, grp, 1 + g, 2 + kind),
                        peer(half, i, rem(j + step, 4)))

    def second_done(grp, g):
        for kind in range(2):
            for half in range(2):
                i, j = pos[half]
                arrived(piece(half, grp, kind, rem(i + OFFSETS[g], 4), rem(j + 2, 4)),
                        f_recv.at[sem(half, grp, 1 + g, 2 + kind)])

    first(0)
    second(0, 0)

    low = nt(tok[...], dwn[...])
    low_hi = low.astype(BF16)
    low_lo = (low - low_hi.astype(F32)).astype(BF16)
    low_swap[c] = nt(dwn[...], tok[...])
    send(low_swap.at[c], low_swap.at[c], l_send.at[0], l_recv.at[c], sib)

    norm_tile.ring_send(norm_tile.core_sum())

    def cot_at(hh, cc, i):
        return cot.at[hh * 2 + cc, :, pl.ds(256 * i, 256)]

    def cot_send(hh, kind, i, dev):
        ref = cot_at(hh, c, i)
        send(ref, ref, k_send.at[kind * 4 + i], k_recv.at[kind * 4 + i], dev)

    for i in range(4):
        cot_send(h, 0, i, tens(fwd))
    arrived(low_swap.at[1 - c], l_recv.at[1 - c])
    own_low = lows.at[h]
    own_low[...] = (low_swap[0] + low_swap[1]).astype(BF16)
    send(own_low, own_low, l_send.at[1], l_recv.at[2 + h], tens(fwd))
    send(own_low, own_low, l_send.at[2], l_recv.at[2 + h], tens(bwd))
    for i in range(4):
        cot_send(h, 1, i, tens(bwd))
    for i in range(4):
        cot_send(h, 3, i, sib)

    first_relay(0)
    second(0, 1)
    second(0, 2)
    second_relay(0, 0)
    first_done(0)
    second(0, 3)

    for k in range(1, 4):
        arrived(weight.at[k, x, y], f_recv.at[k])
    first(1)
    second(1, 0)
    norm_tile.ring_relay()
    second_relay(0, 1)
    second_relay(0, 2)
    first_relay(1)
    second(1, 1)
    second(1, 2)
    second_relay(0, 3)
    for i in range(4):
        arrived(cot_at(bwd, c, i), k_recv.at[i])
        cot_send(bwd, 2, i, tens(fwd))
        cot_send(bwd, 4, i, sib)
    second_relay(1, 0)
    first_done(1)
    second(1, 3)
    arrived(lows.at[bwd], l_recv.at[2 + bwd])
    send(lows.at[bwd], lows.at[bwd], l_send.at[3], l_recv.at[2 + bwd], tens(fwd))
    norm_tile.depth_send(norm_tile.ring_sum())
    second_relay(1, 1)
    second_relay(1, 2)
    norm_tile.plane_send(norm_tile.depth_sum())
    second_relay(1, 3)
    for i in range(4):
        arrived(cot_at(fwd, c, i), k_recv.at[4 + i])
        cot_send(fwd, 5, i, sib)
    for g in range(4):
        for grp in range(2):
            second_done(grp, g)

    def outputs(k):
        return pl.ds(pl.multiple_of(rem(z + k, 4) * 256, 256), 256)

    for k in range(4):
        cols = outputs(k)
        rows = weight[k].reshape(256, 1024)
        out = nt(tok[...], rows) + nn(low_hi, up[:, cols]) + nn(low_lo, up[:, cols])
        part[k] = out.reshape(4, 2, 32, 256)
        swap_out[k] = part[k, :, 1 - c].astype(BF16)
        send(swap_out.at[k], swap_in.at[k], c_send.at[k], c_recv.at[k], sib)

    for i in range(4):
        arrived(cot_at(far, c, i), k_recv.at[8 + i])
        cot_send(far, 6, i, sib)

    for k in range(4):
        arrived(swap_in.at[k], c_recv.at[k])
        pair[k] = part[k, :, c] + swap_in[k].astype(F32)
        hop_out[k, 0] = pair[k, far].astype(BF16)
        send(hop_out.at[k, 0], hop_in.at[k, 0], c_send.at[4 + k], c_recv.at[4 + k], tens(fwd))
    for k in range(4):
        hop_out[k, 1] = pair[k, bwd].astype(BF16)
        send(hop_out.at[k, 1], hop_in.at[k, 1], c_send.at[8 + k], c_recv.at[8 + k], tens(bwd))

    for i in range(4):
        arrived(cot_at(h, 1 - c, i), k_recv.at[12 + i])
        arrived(cot_at(fwd, 1 - c, i), k_recv.at[16 + i])
        arrived(cot_at(bwd, 1 - c, i), k_recv.at[20 + i])
        arrived(cot_at(far, 1 - c, i), k_recv.at[24 + i])

    mg = jnp.zeros((8, 128), F32)
    for k in range(4):
        m = jnp.sum(
            cot[:, :, outputs(k)].reshape(256, 256).astype(F32) * part[k].reshape(256, 256),
            axis=0,
            keepdims=True,
        )
        r = rem(z + k, 4) * 2
        mg = mg + jnp.where(row8 == r, m[:, 0:128], 0.0)
        mg = mg + jnp.where(row8 == r + 1, m[:, 128:256], 0.0)
    mag_tile.core_send(mg)

    norm = jnp.sqrt(norm_tile.plane_sum() + stability_eps)
    fac = mag[...] / norm
    for i in range(8):
        cols = pl.ds(i * 128, 128)
        facrow[:, cols] = fac[i : i + 1, :]
        grad[:, cols] = (
            cot[:, :, cols].reshape(256, 128).astype(F32) * fac[i : i + 1, :]
        ).astype(BF16)
    low_grad = nt(grad[...], up[...]).astype(BF16)
    low_grad_t = nt(up[...], grad[...]).astype(BF16)
    grad_a = nn(low_grad_t, tok[...])
    arrived(lows.at[fwd], l_recv.at[2 + fwd])
    arrived(lows.at[far], l_recv.at[2 + far])
    grad_b = nn(total(lows, 4).astype(BF16), grad[...])
    for q in range(16):
        r, b = q // 8, q % 8
        gb = grad_b[8 * r : 8 * r + 8] if b < 4 else grad_b[16 + 8 * r : 24 + 8 * r]
        gpart[q] = jnp.concatenate(
            [
                grad_a[16 * r : 16 * r + 16, 128 * b : 128 * b + 128],
                gb[:, 128 * b : 128 * b + 128],
                jnp.zeros((8, 128), F32),
            ],
            axis=0,
        ).astype(BF16)
    for k in range(1, 16):
        q = rem(p + k, 16)
        send(gpart.at[q], gplane.at[p], g1_send.at[k - 1], g1_recv.at[p], plane(q))
    gplane[p] = gpart[p]
    mag_tile.plane_send(mag_tile.core_sum())

    tg[...] = (
        sum(nn(grad[:, outputs(k)], weight[k].reshape(256, 1024)) for k in range(4))
        + nn(low_grad, dwn[...])
    ).astype(BF16)
    write(tg, tg_out, 0)

    collect(gplane, p, 16, g1_recv)
    gdepth[z] = total(gplane, 16)[0:24]
    spread(gdepth, z, 4, depth, g2_send, g2_recv)
    mag_tile.depth_send(mag_tile.plane_sum())

    for k in range(4):
        arrived(hop_in.at[k, 0], c_recv.at[4 + k])
        hop_out[k, 2] = (pair[k, fwd] + hop_in[k, 0].astype(F32)).astype(BF16)
        send(hop_out.at[k, 2], hop_in.at[k, 2], c_send.at[12 + k], c_recv.at[12 + k], tens(fwd))

    mag_tile.ring_send(mag_tile.depth_sum())
    collect(gdepth, z, 4, g2_recv)
    gfull[p] = jnp.concatenate([total(gdepth, 4), jnp.zeros((8, 128), F32)], axis=0).astype(BF16)
    spread(gfull, p, 16, plane, g4_send, g4_recv)
    mag_tile.ring_relay()

    for k in range(4):
        cols = outputs(k)
        arrived(hop_in.at[k, 1], c_recv.at[8 + k])
        arrived(hop_in.at[k, 2], c_recv.at[12 + k])
        summed = pair[k, h] + hop_in[k, 1].astype(F32) + hop_in[k, 2].astype(F32)
        proj[:, cols] = (summed * facrow[:, cols]).astype(BF16)
    write(proj, proj_out, 1)

    collect(gfull, p, 16, g4_recv)
    for q in range(16):
        r, b = q // 8, q % 8
        got = gfull[q].astype(F32) * scale
        da[16 * r : 16 * r + 16, 128 * b : 128 * b + 128] = got[0:16]
        lo = 128 * (b % 4)
        db[b // 4, 8 * r : 8 * r + 8, lo : lo + 128] = got[16:24]
    write(da, da_out, 2)
    write(db, db_out, 3)
    mgo[...] = mag_tile.ring_sum() / norm * scale
    write(mgo, mg_out, 4)

    for d in sends:
        d.wait_send()
    for w in writes:
        w.wait()


def finish(*refs):
    for src, dst in zip(refs[:5], refs[5:]):
        dst[...] = src[...]


def body(tokens, frozen, down_factor, up_factor, magnitude, key_value_gradient):
    scale = 1.0 / math.sqrt(tokens.shape[0] * lax.axis_size("dp"))
    dma = pltpu.SemaphoreType.DMA
    hbm = pl.BlockSpec(memory_space=pltpu.HBM)
    vmem = pl.BlockSpec(memory_space=pltpu.VMEM)
    outs = (
        jax.ShapeDtypeStruct((32, 1024), BF16),
        jax.ShapeDtypeStruct((256, 1024), BF16),
        jax.ShapeDtypeStruct((32, 1024), F32),
        jax.ShapeDtypeStruct((2, 16, 512), F32),
        jax.ShapeDtypeStruct((8, 128), F32),
    )
    results = pl.pallas_call(
        functools.partial(kernel, scale),
        out_shape=outs,
        in_specs=[hbm] * 6,
        out_specs=(hbm,) * 5,
        scratch_shapes=[
            pltpu.VMEM((32, 1024), BF16),
            pltpu.VMEM((256, 1024), BF16),
            pltpu.VMEM((32, 1024), F32),
            pltpu.VMEM((2, 16, 512), F32),
            pltpu.VMEM((8, 128), F32),
            pltpu.VMEM((256, 1024), BF16),
            pltpu.VMEM((32, 1024), BF16),
            pltpu.VMEM((8, 128), F32),
            pltpu.VMEM((4, 4, 4, 16, 1024), BF16),
            pltpu.VMEM((8, 32, 1024), BF16),
            pltpu.VMEM((32, 1024), BF16),
            pltpu.VMEM((4, 4, 2, 32, 256), F32),
            pltpu.VMEM((4, 4, 32, 256), F32),
            pltpu.VMEM((256, 1024), BF16),
            pltpu.VMEM((4, 4, 32, 256), BF16),
            pltpu.VMEM((4, 4, 32, 256), BF16),
            pltpu.VMEM((4, 3, 32, 256), BF16),
            pltpu.VMEM((4, 3, 32, 256), BF16),
            pltpu.VMEM((26, 8, 128), F32),
            pltpu.VMEM((26, 8, 128), F32),
            pltpu.VMEM((1, 1024), F32),
            pltpu.VMEM((2, 32, 256), F32),
            pltpu.VMEM((4, 32, 256), BF16),
            pltpu.VMEM((16, 32, 128), BF16),
            pltpu.VMEM((16, 32, 128), BF16),
            pltpu.VMEM((4, 24, 128), F32),
            pltpu.VMEM((16, 32, 128), BF16),
            dma((7,)),
            dma((5,)),
            dma((84,)),
            dma((84,)),
            dma((28,)),
            dma((28,)),
            dma((22,)),
            dma((26,)),
            dma((22,)),
            dma((26,)),
            dma((4,)),
            dma((6,)),
            dma((16,)),
            dma((16,)),
            dma((15,)),
            dma((3,)),
            dma((15,)),
            dma((16,)),
            dma((4,)),
            dma((16,)),
        ],
        compiler_params=pltpu.CompilerParams(
            collective_id=0, has_side_effects=True, vmem_limit_bytes=60 * 1024 * 1024
        ),
        cost_estimate=pl.CostEstimate(
            flops=1200000000, bytes_accessed=2000000, transcendentals=0
        ),
    )(
        tokens,
        frozen,
        down_factor,
        up_factor,
        magnitude.reshape(8, 128),
        key_value_gradient,
    )
    projected, token_gradient, grad_a, grad_b, grad_m = pl.pallas_call(
        finish,
        out_shape=outs,
        in_specs=[vmem] * 5,
        out_specs=(vmem,) * 5,
        compiler_params=pltpu.CompilerParams(vmem_limit_bytes=60 * 1024 * 1024),
    )(*results)
    return projected, token_gradient, grad_a, grad_b, grad_m.reshape(1024)


def solution(mesh):
    placed = (
        P("dp", "tensor"),
        P("dp", "tensor"),
        P(None, "tensor"),
        P(),
        P(),
        P(("dp", "tensor"), None),
    )
    return jax.shard_map(
        body,
        mesh=mesh,
        in_specs=placed,
        out_specs=(P(("dp", "tensor"), None), P("dp", "tensor"), P(None, "tensor"), P(), P()),
        check_vma=False,
    )
```

time: 83.3 us -> 69 us (0.83)
  local copies, waits for them, and re-layouts: 8.22 us -> 0 us
  Pallas kernels: 74 us -> 67.7 us
    unnamed x17 -> x0, local copies, waits for them, and re-layouts: 8.22 us -> none
    pallas_call x1 -> x2, Pallas kernels: 74 us -> 67.7 us  [the longest x1 65.7 us: body(): pl.pallas_call(functools.partial(kernel, scale), out_shape=outs, in_specs...]
where the time goes in v2:
time: 69 us; the launch traced here: 68.3 us
  Pallas kernels  67.7 us (98%)
    pallas_call x1, Pallas kernels, body(): pl.pallas_call(functools.partial(kernel, scale), out_shape=outs, in_specs...  65.7 us
    pallas_call x1, Pallas kernels, body(): pl.pallas_call(finish, out_shape=outs, in_specs=[vmem] * 5, out_specs=(vm...  2.01 us

profile of v2, /device:TPU:1, one launch (start us, length us, event | category | flops | bytes accessed | tf_op | source)
XLA Modules:
  0.0 68.3 jit_solution(9280674906742837728)
XLA Ops:
  0.6 65.7 %shard_map.101 = (bf16[32,1024]{1,0:T(8,128)(2,1)}, bf16[256,1024]{1,0:T(8,128)(2,1)}, f32[32,1024]{1,0:T(8,128)}, f32[2,16,512]{2,1,0:T(8,128)}, f32[8,128]{1,0:T(8,128)}) custom-call(bf16[256,1024]{1,0:T(8,128)(2,1)} %tok_in.1, bf16[16,1024]{1,0:T(8,128)(2,1)} %fro.1, bf16[32,1024]{1,0:T(8,128)(2,1)} %dwn_in.1, bf16[2,16,512]{2,1,0:T(8,128)(2,1)} %upf.1, ...), custom_call_target="tpu_custom_call" | custom-call | flops 1200000000 | bytes 2000000 | tf_op jit(solution)/shard_map/pallas_call | solution.py:536
  66.3 2.0 %shard_map.102 = (bf16[32,1024]{1,0:T(8,128)(2,1)}, bf16[256,1024]{1,0:T(8,128)(2,1)}, f32[32,1024]{1,0:T(8,128)}, f32[2,16,512]{2,1,0:T(8,128)}, f32[8,128]{1,0:T(8,128)}) custom-call(bf16[32,1024]{1,0:T(8,128)(2,1)} %get-tuple-element.15.refs_0_, bf16[256,1024]{1,0:T(8,128)(2,1)} %get-tuple-element.16.refs_1_, f32[32,1024]{1,0:T(8,128)} %get-tuple-element.17.refs_2_, ...), custom_call_target="tpu_custom_call" | custom-call | tf_op jit(solution)/shard_map/pallas_call | solution.py:604

commit v3 on v2

--- a/solution.py
+++ b/solution.py
@@ -63,6 +63,7 @@
     gplane,
     gdepth,
     gfull,
+    met,
     in_sem,
     out_sem,
     f_send,
@@ -106,6 +107,9 @@
     def depth(q):
         return at(q, x, y)
 
+    def column(q):
+        return (rem(q, 4) * 16 + p, lax.div(q, 4) * 2 + c)
+
     def tens(hh):
         return (dp, hh * 2 + c)
 
@@ -223,6 +227,14 @@
         def plane_send(self, value):
             self.buf[10 + p] = value
             spread(self.buf, p, 16, plane, self.ssem, self.rsem, 10, 7)
+
+        def column_send(self, value):
+            self.buf[26 + h * 4 + z] = value
+            spread(self.buf, h * 4 + z, 16, column, self.ssem, self.rsem, 26, 22)
+
+        def column_sum(self):
+            collect(self.buf, h * 4 + z, 16, self.rsem, 26)
+            return total(self.buf, 16, 26)
 
         def plane_sum(self):
             collect(self.buf, p, 16, self.rsem, 10)
@@ -250,6 +262,8 @@
     own_squares = jnp.where(row8 == lax.div(dp, 8), line, 0.0)
 
     pl.semaphore_wait(barrier, 21)
+    for hh in (fwd, bwd):
+        pl.semaphore_signal(met.at[0], inc=1, device_id=tens(hh), device_id_type=MESH)
 
     own_rows = weight.at[0, x, y]
     for k in range(1, 4):
@@ -257,18 +271,15 @@
              depth(rem(z + k, 4)))
     norm_tile.core_send(own_squares)
 
-    slots = (pl.ds(0, 1), pl.ds(1, 3))
     pos = ((x, y), (y, x))
 
-    def block(half, grp, i, j, lo, wide):
+    def unit(half, grp, i, j):
         i, j = (i, j) if half == 0 else (j, i)
-        return weight.at[slots[grp], i, j, :, pl.ds(half * 512 + lo, wide)]
-
-    def unit(half, grp, i, j):
-        return block(half, grp, i, j, 0, 512)
+        return weight.at[pl.ds(2 * half, 2), i, j]
 
     def piece(half, grp, kind, i, j):
-        return block(half, grp, i, j, 256 * kind, 256)
+        i, j = (i, j) if half == 0 else (j, i)
+        return weight.at[2 * half + kind, i, j]
 
     def peer(half, i, j):
         return at(z, i, j) if half == 0 else at(z, j, i)
@@ -326,74 +337,61 @@
                 arrived(piece(half, grp, kind, rem(i + OFFSETS[g], 4), rem(j + 2, 4)),
                         f_recv.at[sem(half, grp, 1 + g, 2 + kind)])
 
-    first(0)
-    second(0, 0)
-
+
+    low_swap[c] = nt(dwn[...], tok[...])
+    send(low_swap.at[c], low_swap.at[c], l_send.at[0], l_recv.at[c], sib)
     low = nt(tok[...], dwn[...])
     low_hi = low.astype(BF16)
     low_lo = (low - low_hi.astype(F32)).astype(BF16)
-    low_swap[c] = nt(dwn[...], tok[...])
-    send(low_swap.at[c], low_swap.at[c], l_send.at[0], l_recv.at[c], sib)
 
     norm_tile.ring_send(norm_tile.core_sum())
 
     def cot_at(hh, cc, i):
-        return cot.at[hh * 2 + cc, :, pl.ds(256 * i, 256)]
+        return cot.at[hh * 2 + cc, :, pl.ds(512 * i, 512)]
 
     def cot_send(hh, kind, i, dev):
         ref = cot_at(hh, c, i)
         send(ref, ref, k_send.at[kind * 4 + i], k_recv.at[kind * 4 + i], dev)
 
-    for i in range(4):
+    def cot_relay(i):
+        arrived(cot_at(bwd, c, i), k_recv.at[i])
+        cot_send(bwd, 2, i, tens(fwd))
+        cot_send(bwd, 4, i, sib)
+
+    for k in range(1, 4):
+        arrived(weight.at[k, x, y], f_recv.at[k])
+    first(1)
+    second(1, 0)
+    norm_tile.ring_relay()
+    for i in range(2):
         cot_send(h, 0, i, tens(fwd))
+    for i in range(2):
+        cot_send(h, 1, i, tens(bwd))
+    for i in range(2):
+        cot_send(h, 3, i, sib)
     arrived(low_swap.at[1 - c], l_recv.at[1 - c])
     own_low = lows.at[h]
     own_low[...] = (low_swap[0] + low_swap[1]).astype(BF16)
     send(own_low, own_low, l_send.at[1], l_recv.at[2 + h], tens(fwd))
     send(own_low, own_low, l_send.at[2], l_recv.at[2 + h], tens(bwd))
-    for i in range(4):
-        cot_send(h, 1, i, tens(bwd))
-    for i in range(4):
-        cot_send(h, 3, i, sib)
-
-    first_relay(0)
-    second(0, 1)
-    second(0, 2)
-    second_relay(0, 0)
-    first_done(0)
-    second(0, 3)
-
-    for k in range(1, 4):
-        arrived(weight.at[k, x, y], f_recv.at[k])
-    first(1)
-    second(1, 0)
-    norm_tile.ring_relay()
-    second_relay(0, 1)
-    second_relay(0, 2)
+    pl.semaphore_wait(met.at[0], 2)
+    for hh in (fwd, bwd):
+        pl.semaphore_signal(met.at[1], inc=1, device_id=tens(hh), device_id_type=MESH)
     first_relay(1)
     second(1, 1)
     second(1, 2)
-    second_relay(0, 3)
-    for i in range(4):
-        arrived(cot_at(bwd, c, i), k_recv.at[i])
-        cot_send(bwd, 2, i, tens(fwd))
-        cot_send(bwd, 4, i, sib)
     second_relay(1, 0)
     first_done(1)
     second(1, 3)
-    arrived(lows.at[bwd], l_recv.at[2 + bwd])
-    send(lows.at[bwd], lows.at[bwd], l_send.at[3], l_recv.at[2 + bwd], tens(fwd))
     norm_tile.depth_send(norm_tile.ring_sum())
     second_relay(1, 1)
     second_relay(1, 2)
+    cot_relay(0)
+    second_relay(1, 3)
+    cot_relay(1)
     norm_tile.plane_send(norm_tile.depth_sum())
-    second_relay(1, 3)
-    for i in range(4):
-        arrived(cot_at(fwd, c, i), k_recv.at[4 + i])
-        cot_send(fwd, 5, i, sib)
     for g in range(4):
-        for grp in range(2):
-            second_done(grp, g)
+        second_done(1, g)
 
     def outputs(k):
         return pl.ds(pl.multiple_of(rem(z + k, 4) * 256, 256), 256)
@@ -406,9 +404,12 @@
         swap_out[k] = part[k, :, 1 - c].astype(BF16)
         send(swap_out.at[k], swap_in.at[k], c_send.at[k], c_recv.at[k], sib)
 
-    for i in range(4):
-        arrived(cot_at(far, c, i), k_recv.at[8 + i])
-        cot_send(far, 6, i, sib)
+    for i in range(2):
+        arrived(cot_at(fwd, c, i), k_recv.at[4 + i])
+        cot_send(fwd, 5, i, sib)
+
+    arrived(lows.at[bwd], l_recv.at[2 + bwd])
+    send(lows.at[bwd], lows.at[bwd], l_send.at[3], l_recv.at[2 + bwd], tens(fwd))
 
     for k in range(4):
         arrived(swap_in.at[k], c_recv.at[k])
@@ -419,7 +420,10 @@
         hop_out[k, 1] = pair[k, bwd].astype(BF16)
         send(hop_out.at[k, 1], hop_in.at[k, 1], c_send.at[8 + k], c_recv.at[8 + k], tens(bwd))
 
-    for i in range(4):
+    for i in range(2):
+        arrived(cot_at(far, c, i), k_recv.at[8 + i])
+        cot_send(far, 6, i, sib)
+    for i in range(2):
         arrived(cot_at(h, 1 - c, i), k_recv.at[12 + i])
         arrived(cot_at(fwd, 1 - c, i), k_recv.at[16 + i])
         arrived(cot_at(bwd, 1 - c, i), k_recv.at[20 + i])
@@ -436,6 +440,20 @@
         mg = mg + jnp.where(row8 == r, m[:, 0:128], 0.0)
         mg = mg + jnp.where(row8 == r + 1, m[:, 128:256], 0.0)
     mag_tile.core_send(mg)
+
+    pl.semaphore_wait(met.at[1], 2)
+    mag_tile.plane_send(mag_tile.core_sum())
+    def hop_relay(k):
+        arrived(hop_in.at[k, 0], c_recv.at[4 + k])
+        hop_out[k, 2] = (pair[k, fwd] + hop_in[k, 0].astype(F32)).astype(BF16)
+        send(hop_out.at[k, 2], hop_in.at[k, 2], c_send.at[12 + k], c_recv.at[12 + k], tens(fwd))
+
+    def hop_last(k):
+        cols = outputs(k)
+        arrived(hop_in.at[k, 1], c_recv.at[8 + k])
+        arrived(hop_in.at[k, 2], c_recv.at[12 + k])
+        summed = pair[k, h] + hop_in[k, 1].astype(F32) + hop_in[k, 2].astype(F32)
+        proj[:, cols] = (summed * facrow[:, cols]).astype(BF16)
 
     norm = jnp.sqrt(norm_tile.plane_sum() + stability_eps)
     fac = mag[...] / norm
@@ -466,7 +484,6 @@
         q = rem(p + k, 16)
         send(gpart.at[q], gplane.at[p], g1_send.at[k - 1], g1_recv.at[p], plane(q))
     gplane[p] = gpart[p]
-    mag_tile.plane_send(mag_tile.core_sum())
 
     tg[...] = (
         sum(nn(grad[:, outputs(k)], weight[k].reshape(256, 1024)) for k in range(4))
@@ -474,28 +491,22 @@
     ).astype(BF16)
     write(tg, tg_out, 0)
 
+    mag_tile.column_send(mag_tile.plane_sum())
+    hop_relay(0)
+    hop_relay(1)
     collect(gplane, p, 16, g1_recv)
     gdepth[z] = total(gplane, 16)[0:24]
     spread(gdepth, z, 4, depth, g2_send, g2_recv)
-    mag_tile.depth_send(mag_tile.plane_sum())
-
-    for k in range(4):
-        arrived(hop_in.at[k, 0], c_recv.at[4 + k])
-        hop_out[k, 2] = (pair[k, fwd] + hop_in[k, 0].astype(F32)).astype(BF16)
-        send(hop_out.at[k, 2], hop_in.at[k, 2], c_send.at[12 + k], c_recv.at[12 + k], tens(fwd))
-
-    mag_tile.ring_send(mag_tile.depth_sum())
+    hop_relay(2)
+    hop_relay(3)
+
     collect(gdepth, z, 4, g2_recv)
     gfull[p] = jnp.concatenate([total(gdepth, 4), jnp.zeros((8, 128), F32)], axis=0).astype(BF16)
     spread(gfull, p, 16, plane, g4_send, g4_recv)
-    mag_tile.ring_relay()
-
-    for k in range(4):
-        cols = outputs(k)
-        arrived(hop_in.at[k, 1], c_recv.at[8 + k])
-        arrived(hop_in.at[k, 2], c_recv.at[12 + k])
-        summed = pair[k, h] + hop_in[k, 1].astype(F32) + hop_in[k, 2].astype(F32)
-        proj[:, cols] = (summed * facrow[:, cols]).astype(BF16)
+    hop_last(0)
+    hop_last(1)
+    hop_last(2)
+    hop_last(3)
     write(proj, proj_out, 1)
 
     collect(gfull, p, 16, g4_recv)
@@ -507,7 +518,7 @@
         db[b // 4, 8 * r : 8 * r + 8, lo : lo + 128] = got[16:24]
     write(da, da_out, 2)
     write(db, db_out, 3)
-    mgo[...] = mag_tile.ring_sum() / norm * scale
+    mgo[...] = mag_tile.column_sum() / norm * scale
     write(mgo, mg_out, 4)
 
     for d in sends:
@@ -558,7 +569,7 @@
             pltpu.VMEM((4, 3, 32, 256), BF16),
             pltpu.VMEM((4, 3, 32, 256), BF16),
             pltpu.VMEM((26, 8, 128), F32),
-            pltpu.VMEM((26, 8, 128), F32),
+            pltpu.VMEM((42, 8, 128), F32),
             pltpu.VMEM((1, 1024), F32),
             pltpu.VMEM((2, 32, 256), F32),
             pltpu.VMEM((4, 32, 256), BF16),
@@ -566,6 +577,7 @@
             pltpu.VMEM((16, 32, 128), BF16),
             pltpu.VMEM((4, 24, 128), F32),
             pltpu.VMEM((16, 32, 128), BF16),
+            pltpu.SemaphoreType.REGULAR((2,)),
             dma((7,)),
             dma((5,)),
             dma((84,)),
@@ -574,8 +586,8 @@
             dma((28,)),
             dma((22,)),
             dma((26,)),
-            dma((22,)),
-            dma((26,)),
+            dma((37,)),
+            dma((42,)),
             dma((4,)),
             dma((6,)),
             dma((16,)),

time: 69 us -> 65.4 us (0.948)
  the two profiles are of different devices: /device:TPU:1 before, /device:TPU:8 now
where the time goes in v3:
time: 65.4 us; the launch traced here: 65.2 us
  Pallas kernels  64.6 us (99%)
    pallas_call x1, Pallas kernels, body(): pl.pallas_call(functools.partial(kernel, scale), out_shape=outs, in_specs...  62.6 us
    pallas_call x1, Pallas kernels, body(): pl.pallas_call(finish, out_shape=outs, in_specs=[vmem] * 5, out_specs=(vm...  2.01 us

profile of v3, /device:TPU:8, one launch (start us, length us, event | category | flops | bytes accessed | tf_op | source)
XLA Modules:
  0.0 65.2 jit_solution(4782321692817715417)
XLA Ops:
  0.6 62.6 %shard_map.101 = (bf16[32,1024]{1,0:T(8,128)(2,1)}, bf16[256,1024]{1,0:T(8,128)(2,1)}, f32[32,1024]{1,0:T(8,128)}, f32[2,16,512]{2,1,0:T(8,128)}, f32[8,128]{1,0:T(8,128)}) custom-call(bf16[256,1024]{1,0:T(8,128)(2,1)} %tok_in.1, bf16[16,1024]{1,0:T(8,128)(2,1)} %fro.1, bf16[32,1024]{1,0:T(8,128)(2,1)} %dwn_in.1, bf16[2,16,512]{2,1,0:T(8,128)(2,1)} %upf.1, ...), custom_call_target="tpu_custom_call" | custom-call | flops 1200000000 | bytes 2000000 | tf_op jit(solution)/shard_map/pallas_call | solution.py:547
  63.2 2.0 %shard_map.102 = (bf16[32,1024]{1,0:T(8,128)(2,1)}, bf16[256,1024]{1,0:T(8,128)(2,1)}, f32[32,1024]{1,0:T(8,128)}, f32[2,16,512]{2,1,0:T(8,128)}, f32[8,128]{1,0:T(8,128)}) custom-call(bf16[32,1024]{1,0:T(8,128)(2,1)} %get-tuple-element.15.refs_0_, bf16[256,1024]{1,0:T(8,128)(2,1)} %get-tuple-element.16.refs_1_, f32[32,1024]{1,0:T(8,128)} %get-tuple-element.17.refs_2_, ...), custom_call_target="tpu_custom_call" | custom-call | tf_op jit(solution)/shard_map/pallas_call | solution.py:616

commit v4 on v3

--- a/solution.py
+++ b/solution.py
@@ -384,11 +384,11 @@
     first_done(1)
     second(1, 3)
     norm_tile.depth_send(norm_tile.ring_sum())
+    cot_relay(0)
     second_relay(1, 1)
     second_relay(1, 2)
-    cot_relay(0)
+    cot_relay(1)
     second_relay(1, 3)
-    cot_relay(1)
     norm_tile.plane_send(norm_tile.depth_sum())
     for g in range(4):
         second_done(1, g)
@@ -402,7 +402,9 @@
         out = nt(tok[...], rows) + nn(low_hi, up[:, cols]) + nn(low_lo, up[:, cols])
         part[k] = out.reshape(4, 2, 32, 256)
         swap_out[k] = part[k, :, 1 - c].astype(BF16)
-        send(swap_out.at[k], swap_in.at[k], c_send.at[k], c_recv.at[k], sib)
+        if k % 2:
+            two = pl.ds(k - 1, 2)
+            send(swap_out.at[two], swap_in.at[two], c_send.at[k // 2], c_recv.at[k // 2], sib)
 
     for i in range(2):
         arrived(cot_at(fwd, c, i), k_recv.at[4 + i])
@@ -411,14 +413,24 @@
     arrived(lows.at[bwd], l_recv.at[2 + bwd])
     send(lows.at[bwd], lows.at[bwd], l_send.at[3], l_recv.at[2 + bwd], tens(fwd))
 
-    for k in range(4):
-        arrived(swap_in.at[k], c_recv.at[k])
-        pair[k] = part[k, :, c] + swap_in[k].astype(F32)
-        hop_out[k, 0] = pair[k, far].astype(BF16)
-        send(hop_out.at[k, 0], hop_in.at[k, 0], c_send.at[4 + k], c_recv.at[4 + k], tens(fwd))
-    for k in range(4):
-        hop_out[k, 1] = pair[k, bwd].astype(BF16)
-        send(hop_out.at[k, 1], hop_in.at[k, 1], c_send.at[8 + k], c_recv.at[8 + k], tens(bwd))
+    def hop_send(m, kind, dev):
+        two = pl.ds(2 * m, 2)
+        s = 4 * (kind + 1) + m
+        send(hop_out.at[two, kind], hop_in.at[two, kind], c_send.at[s], c_recv.at[s], dev)
+
+    def hop_arrived(m, kind):
+        arrived(hop_in.at[pl.ds(2 * m, 2), kind], c_recv.at[4 * (kind + 1) + m])
+
+    for m in range(2):
+        arrived(swap_in.at[pl.ds(2 * m, 2)], c_recv.at[m])
+        for k in (2 * m, 2 * m + 1):
+            pair[k] = part[k, :, c] + swap_in[k].astype(F32)
+            hop_out[k, 0] = pair[k, far].astype(BF16)
+        hop_send(m, 0, tens(fwd))
+    for m in range(2):
+        for k in (2 * m, 2 * m + 1):
+            hop_out[k, 1] = pair[k, bwd].astype(BF16)
+        hop_send(m, 1, tens(bwd))
 
     for i in range(2):
         arrived(cot_at(far, c, i), k_recv.at[8 + i])
@@ -443,15 +455,17 @@
 
     pl.semaphore_wait(met.at[1], 2)
     mag_tile.plane_send(mag_tile.core_sum())
-    def hop_relay(k):
-        arrived(hop_in.at[k, 0], c_recv.at[4 + k])
-        hop_out[k, 2] = (pair[k, fwd] + hop_in[k, 0].astype(F32)).astype(BF16)
-        send(hop_out.at[k, 2], hop_in.at[k, 2], c_send.at[12 + k], c_recv.at[12 + k], tens(fwd))
+    def hop_relay(m):
+        hop_arrived(m, 0)
+        for k in (2 * m, 2 * m + 1):
+            hop_out[k, 2] = (pair[k, fwd] + hop_in[k, 0].astype(F32)).astype(BF16)
+        hop_send(m, 2, tens(fwd))
 
     def hop_last(k):
         cols = outputs(k)
-        arrived(hop_in.at[k, 1], c_recv.at[8 + k])
-        arrived(hop_in.at[k, 2], c_recv.at[12 + k])
+        if k % 2 == 0:
+            hop_arrived(k // 2, 1)
+            hop_arrived(k // 2, 2)
         summed = pair[k, h] + hop_in[k, 1].astype(F32) + hop_in[k, 2].astype(F32)
         proj[:, cols] = (summed * facrow[:, cols]).astype(BF16)
 
@@ -493,12 +507,10 @@
 
     mag_tile.column_send(mag_tile.plane_sum())
     hop_relay(0)
-    hop_relay(1)
     collect(gplane, p, 16, g1_recv)
     gdepth[z] = total(gplane, 16)[0:24]
     spread(gdepth, z, 4, depth, g2_send, g2_recv)
-    hop_relay(2)
-    hop_relay(3)
+    hop_relay(1)
 
     collect(gdepth, z, 4, g2_recv)
     gfull[p] = jnp.concatenate([total(gdepth, 4), jnp.zeros((8, 128), F32)], axis=0).astype(BF16)

time: 65.4 us -> 64.6 us (0.988)
  the two profiles are of different devices: /device:TPU:8 before, /device:TPU:1 now
where the time goes in v4:
time: 64.6 us; the launch traced here: 63.6 us
  Pallas kernels  63 us (98%)
    pallas_call x1, Pallas kernels, body(): pl.pallas_call(functools.partial(kernel, scale), out_shape=outs, in_specs...  61 us
    pallas_call x1, Pallas kernels, body(): pl.pallas_call(finish, out_shape=outs, in_specs=[vmem] * 5, out_specs=(vm...  2.01 us

profile of v4, /device:TPU:1, one launch (start us, length us, event | category | flops | bytes accessed | tf_op | source)
XLA Modules:
  0.0 63.6 jit_solution(4824120700370882408)
XLA Ops:
  0.6 61.0 %shard_map.101 = (bf16[32,1024]{1,0:T(8,128)(2,1)}, bf16[256,1024]{1,0:T(8,128)(2,1)}, f32[32,1024]{1,0:T(8,128)}, f32[2,16,512]{2,1,0:T(8,128)}, f32[8,128]{1,0:T(8,128)}) custom-call(bf16[256,1024]{1,0:T(8,128)(2,1)} %tok_in.1, bf16[16,1024]{1,0:T(8,128)(2,1)} %fro.1, bf16[32,1024]{1,0:T(8,128)(2,1)} %dwn_in.1, bf16[2,16,512]{2,1,0:T(8,128)(2,1)} %upf.1, ...), custom_call_target="tpu_custom_call" | custom-call | flops 1200000000 | bytes 2000000 | tf_op jit(solution)/shard_map/pallas_call | solution.py:559
  61.6 2.0 %shard_map.102 = (bf16[32,1024]{1,0:T(8,128)(2,1)}, bf16[256,1024]{1,0:T(8,128)(2,1)}, f32[32,1024]{1,0:T(8,128)}, f32[2,16,512]{2,1,0:T(8,128)}, f32[8,128]{1,0:T(8,128)}) custom-call(bf16[32,1024]{1,0:T(8,128)(2,1)} %get-tuple-element.15.refs_0_, bf16[256,1024]{1,0:T(8,128)(2,1)} %get-tuple-element.16.refs_1_, f32[32,1024]{1,0:T(8,128)} %get-tuple-element.17.refs_2_, ...), custom_call_target="tpu_custom_call" | custom-call | tf_op jit(solution)/shard_map/pallas_call | solution.py:628
